TPU v7x, 512 devices: a whole 4x4x16 slice. The times are simulated.
512 devices in a mesh: row: 64 (over z, x), col: 8 (over y, core).
Axes of the slice: x: 4, y: 4, z: 16, core: 2. Of those that a mesh axis runs over, the one named last changes fastest.
Arguments:
- half_tensor: float32 [64, 400, 4096], P('row', 'col'), may hold values from -0.0390625 to 0.0390625
- earlier_blocks: float32 [64, 512, 512], P('row'), may hold values from -6 to 6
Outputs:
- exchange_blocks: float32 [64, 512, 512], P('row')
All inputs are finite; a program needn't handle non-finite values.
Results may differ from a plain program's by a relative error of at most 0.000068.
Values sent between devices are 32-bit elements; how exact they have to be, the bound alone decides.
A program may use at most 128 MiB of HBM per device.

v0:
```python
import math

import jax
import jax.numpy as jnp
from jax import lax
from jax.sharding import PartitionSpec as P


def body(half_tensor, earlier_blocks):
    grid_side = math.isqrt(lax.axis_size("row"))
    aux_dev, occ_dev, basis = half_tensor.shape
    width = basis // grid_side
    first_groups = jnp.broadcast_to(
        half_tensor.reshape(aux_dev, occ_dev, grid_side, 1, width),
        (aux_dev, occ_dev, grid_side, grid_side, width),
    ).reshape(aux_dev, occ_dev, grid_side * grid_side, width)
    second_groups = jnp.broadcast_to(
        half_tensor.reshape(aux_dev, occ_dev, 1, grid_side, width),
        (aux_dev, occ_dev, grid_side, grid_side, width),
    ).reshape(aux_dev, occ_dev, grid_side * grid_side, width)
    row_whole = lax.all_to_all(first_groups, "row", split_axis=2, concat_axis=0, tiled=True)[
        :, :, 0, :
    ]
    partial_block = jnp.einsum(
        "pom,poxn->mn",
        row_whole,
        lax.all_to_all(second_groups, "row", split_axis=2, concat_axis=0, tiled=True),
        preferred_element_type=jnp.float32,
        precision=lax.Precision.HIGHEST,
    )
    summed = lax.psum(partial_block, "col")
    result = earlier_blocks[0] + summed
    return result[None]


def solution(mesh):
    return jax.shard_map(
        body,
        mesh=mesh,
        in_specs=(P("row", "col", None), P("row", None, None)),
        out_specs=P("row", None, None),
        check_vma=False,
    )
```

profile of v0, /device:TPU:1, one launch (start us, length us, event | category | flops | bytes accessed | tf_op | source)
XLA Modules:
  0.0 723.7 jit_solution(17482193992639745656)
XLA Ops:
  6.5 3.1 reduce
  9.6 0.5 copy.15
  10.2 0.1 slice
  10.2 4.5 broadcast_bitcast_fusion.1
  14.7 7.9 %copy.11 = f32[1,50,64,512]{3,0,1,2:T(1,128)} copy(f32[1,50,64,512]{3,2,1,0:T(8,128)S(1)} %get-tuple-element.5) | data formatting | bytes 13107200 | tf_op jit(solution)/shard_map/broadcast_in_dim | solution.py:13
  22.6 19.3 %all-to-all-start = ((f32[1,50,64,512]{3,0,1,2:T(1,128)}), f32[1,50,64,512]{3,0,1,2:T(1,128)}, u32[]{:S(2)}, u32[]{:S(2)}) async-start(f32[1,50,64,512]{3,0,1,2:T(1,128)} %copy.11), calls=%async_computation | async-start | bytes 13107200 | tf_op jit(solution)/shard_map/all_to_all | solution.py:21
  42.0 0.0 all-reduce.2.cloned.1.call-start
  42.0 9.2 %copy.13 = f32[1,50,64,512]{3,0,1,2:T(1,128)} copy(f32[1,50,64,512]{3,2,1,0:T(8,128)} %get-tuple-element.6) | data formatting | bytes 13107200 | tf_op jit(solution)/shard_map/broadcast_in_dim | solution.py:17
  51.3 274.0 %all-to-all-done = f32[1,50,64,512]{3,0,1,2:T(1,128)} async-done(((f32[1,50,64,512]{3,0,1,2:T(1,128)}), f32[1,50,64,512]{3,0,1,2:T(1,128)}, u32[]{:S(2)}, u32[]{:S(2)}) %all-to-all-start) | async-done | bytes 6553632 | tf_op jit(solution)/shard_map/all_to_all | solution.py:21
  325.3 301.6 %all_to_all.30 = f32[1,50,64,512]{3,0,1,2:T(1,128)S(1)} all-to-all(f32[1,50,64,512]{3,0,1,2:T(1,128)} %copy.13), channel_id=1, replica_groups=mesh['row'=64,'col'=8] {'row'}, dimensions={2} | all-to-all | bytes 13107200 | tf_op jit(solution)/shard_map/all_to_all | solution.py:27
  626.9 0.0 copy-start
  626.9 16.4 %fusion.5 = f32[512,512]{1,0:T(8,128)} fusion(f32[1,50,64,512]{3,0,1,2:T(1,128)S(1)} %all_to_all.30, f32[1,50,64,512]{3,0,1,2:T(1,128)} %all-to-all-done), kind=kOutput, calls=%fused_computation.7 | convolution fusion | flops 10066329600 | bytes 14155776 | tf_op jit(solution)/shard_map/pom,poxn->mn/dot_general | solution.py:24
  643.2 0.0 all-reduce.2.cloned.1.call-update
  643.3 71.2 %all-reduce.2.cloned.1.call-done = f32[512,512]{1,0:T(8,128)} async-done(((f32[512,512]{1,0:T(8,128)}), f32[512,512]{1,0:T(8,128)}) %all-reduce.2.cloned.1.call-update) | async-done | bytes 1048592 | tf_op jit(solution)/shard_map/psum | solution.py:31
  714.5 0.0 copy-done
  714.5 2.4 fusion.10
Async XLA Ops:
  22.6 302.7 %all-to-all-start = ((f32[1,50,64,512]{3,0,1,2:T(1,128)}), f32[1,50,64,512]{3,0,1,2:T(1,128)}, u32[]{:S(2)}, u32[]{:S(2)}) async-start(f32[1,50,64,512]{3,0,1,2:T(1,128)} %copy.11), calls=%async_computation | async-start | bytes 13107200 | tf_op jit(solution)/shard_map/all_to_all | solution.py:21
  42.0 672.5 %all-reduce.2.cloned.1.call-start = ((), (), s32[]{:S(2)}) async-start(), calls=%async_computation.2 | async-start | bytes 2097152 | tf_op jit(solution)/shard_map/psum | solution.py:31
  626.9 87.6 %copy-start = (f32[1,512,512]{2,1,0:T(8,128)S(1)}, f32[1,512,512]{2,1,0:T(8,128)}, u32[]{:S(2)}) copy-start(f32[1,512,512]{2,1,0:T(8,128)} %param.3) | copy-start | bytes 3145732
Sparse Core Ops, SparseCore 0:
  643.4 71.0 all-reduce.1
where the time goes:
time: 725 us; the launch traced here: 724 us
  waiting for transfers between devices  345 us (48%)
  blocking collectives  302 us (42%)
  local copies, waits for them, and re-layouts  22.2 us (3%)
  starting transfers between devices  19.4 us (3%)
  matrix products  16.4 us (2%)
  between operations  13.4 us (2%)
    all_to_all x1, blocking collectives, body(): lax.all_to_all(second_groups, 'row', split_axis=2, concat_axis=0, tiled=T...  302 us
    all_to_all x1, waiting for transfers between devices, body(): lax.all_to_all(first_groups, 'row', split_axis=2, concat_axis=0, tiled=True)  274 us
    psum x1, waiting for transfers between devices, body(): summed = lax.psum(partial_block, 'col')  71.2 us
    all_to_all x1, starting transfers between devices, body(): lax.all_to_all(first_groups, 'row', split_axis=2, concat_axis=0, tiled=True)  19.3 us
    dot_general x1, matrix products, body(): jnp.einsum('pom,poxn->mn', row_whole, lax.all_to_all(second_groups, 'row'...  16.4 us
  transfers between devices with their start and end apart: 2, of which 2 were waited for; matrix products, arithmetic and copies ran while one was open for 1% of the time, Pallas kernels for 0%

commit v1 on v0

v1 whole, which is shorter than its diff:
```python
import jax
import jax.numpy as jnp
from jax import lax
from jax.experimental import pallas as pl
from jax.experimental.pallas import tpu as pltpu
from jax.sharding import PartitionSpec as P

MESH = pl.DeviceIdType.MESH
F32 = jnp.float32
BF16 = jnp.bfloat16

NX, NY, NZ, NK = 4, 4, 16, 2
ROWS = 50
PIECE = ROWS * 8
DEPTH = 16 * ROWS
PADDED = 896
HALF = 25 * 8
QUARTER = 128
OWN = 64
WIDTH = 512


def kernel(
    half_ref,
    earlier_ref,
    out_ref,
    col_send,
    row_send,
    col_buf,
    row_buf,
    row_hi,
    row_lo,
    col_hi,
    col_lo,
    tile,
    sibling_tile,
    up_send,
    down_send,
    up_recv,
    down_recv,
    c_ssem,
    c_rsem,
    r_ssem,
    r_rsem,
    s_ssem,
    s_rsem,
    up_ssem,
    up_rsem,
    down_ssem,
    down_rsem,
    o_ssem,
    o_rsem,
):
    r = lax.axis_index("row")
    c = lax.axis_index("col")
    z, x, y, k = r // NX, r % NX, c // NK, c % NK

    def device(dz=0, dx=0, dy=0, dk=0):
        return (
            lax.rem(z + dz, NZ) * NX + lax.rem(x + dx, NX),
            lax.rem(y + dy, NY) * NK + lax.rem(k + dk, NK),
        )

    def remote(src, dst, ssem, rsem, to):
        return pltpu.make_async_remote_copy(
            src_ref=src, dst_ref=dst, send_sem=ssem, recv_sem=rsem, device_id=to, device_id_type=MESH
        )

    peers = [device(dx=j) for j in range(1, NX)] + [device(dy=j) for j in range(1, NY)]
    peers += [device(dz=1), device(dz=NZ - 1), device(dk=1)]
    barrier = pltpu.get_barrier_semaphore()
    for peer in peers:
        pl.semaphore_signal(barrier, inc=1, device_id=peer, device_id_type=MESH)

    for i in range(7):
        n = min(8, ROWS - 8 * i)
        for t in range(32):
            g, q = t // 4, t % 4
            v = half_ref[0, 8 * i : 8 * i + n, 128 * t : 128 * t + 128]
            col_send[g % 4, pl.ds(64 * i + (g // 4) * 4 + q, n, stride=8), :] = v
            row_send[q, pl.ds(64 * i + g, n, stride=8), :] = v
    col_buf[pl.ds(0, PIECE), :] = col_send[x]
    row_buf[pl.ds(0, PIECE), :] = row_send[y]
    pad = jnp.zeros((8 * (PADDED - DEPTH), 128), F32)
    col_buf[pl.ds(8 * DEPTH, 8 * (PADDED - DEPTH)), :] = pad
    row_buf[pl.ds(8 * DEPTH, 8 * (PADDED - DEPTH)), :] = pad

    pl.semaphore_wait(barrier, len(peers))

    def slot(buf, dx, dy, part=None):
        base = (dx * 4 + dy) * PIECE
        if part is None:
            return buf.at[pl.ds(base, PIECE), :]
        return buf.at[pl.ds(base + part * HALF, HALF), :]

    sends = []

    def go(copy):
        copy.start()
        sends.append(copy)

    for j in (1, 3, 2):
        go(remote(col_send.at[lax.rem(x + j, NX)], slot(col_buf, 4 - j, 0), c_ssem.at[j, 0], c_rsem.at[4 - j, 0], device(dx=j)))
        go(remote(row_send.at[lax.rem(y + j, NY)], slot(row_buf, 0, 4 - j), r_ssem.at[j, 0], r_rsem.at[0, 4 - j], device(dy=j)))

    def spread(a):
        go(remote(slot(col_buf, a, 0), slot(col_buf, a, 3), c_ssem.at[a, 1], c_rsem.at[a, 3], device(dy=1)))
        go(remote(slot(row_buf, 0, a), slot(row_buf, 3, a), r_ssem.at[a, 1], r_rsem.at[3, a], device(dx=1)))
        go(remote(slot(col_buf, a, 0), slot(col_buf, a, 1), c_ssem.at[a, 2], c_rsem.at[a, 1], device(dy=3)))
        go(remote(slot(row_buf, 0, a), slot(row_buf, 1, a), r_ssem.at[a, 2], r_rsem.at[1, a], device(dx=3)))

    def arrived(dst, rsem):
        remote(dst, dst, rsem, rsem, device(dy=1)).wait_recv()

    def forward(a):
        arrived(slot(col_buf, a, 3), c_rsem.at[a, 3])
        go(remote(slot(col_buf, a, 3, 0), slot(col_buf, a, 2, 0), c_ssem.at[a, 3], c_rsem.at[a, 2], device(dy=1)))
        arrived(slot(row_buf, 3, a), r_rsem.at[3, a])
        go(remote(slot(row_buf, 3, a, 0), slot(row_buf, 2, a, 0), r_ssem.at[a, 3], r_rsem.at[2, a], device(dx=1)))
        arrived(slot(col_buf, a, 1), c_rsem.at[a, 1])
        go(remote(slot(col_buf, a, 1, 1), slot(col_buf, a, 2, 1), c_ssem.at[a, 4], c_rsem.at[a, 4], device(dy=3)))
        arrived(slot(row_buf, 1, a), r_rsem.at[1, a])
        go(remote(slot(row_buf, 1, a, 1), slot(row_buf, 2, a, 1), r_ssem.at[a, 4], r_rsem.at[4, a], device(dx=3)))

    spread(0)
    for a in (3, 1, 2):
        arrived(slot(col_buf, a, 0), c_rsem.at[a, 0])
        arrived(slot(row_buf, 0, a), r_rsem.at[0, a])
        spread(a)
        if a == 3:
            forward(0)
    for a in (3, 1, 2):
        forward(a)
    for a in range(4):
        arrived(slot(col_buf, a, 2, 0), c_rsem.at[a, 2])
        arrived(slot(row_buf, 2, a, 0), r_rsem.at[2, a])
        arrived(slot(col_buf, a, 2, 1), c_rsem.at[a, 4])
        arrived(slot(row_buf, 2, a, 1), r_rsem.at[4, a])

    for s in range(8):
        v = col_buf[pl.ds(s, PADDED, stride=8), :]
        hi = v.astype(BF16)
        col_hi[:, 128 * s : 128 * s + 128] = hi
        col_lo[:, 128 * s : 128 * s + 128] = (v - hi.astype(F32)).astype(BF16)
        v = row_buf[pl.ds(s, PADDED, stride=8), :].T
        hi = v.astype(BF16)
        row_hi[128 * s : 128 * s + 128, :] = hi
        row_lo[128 * s : 128 * s + 128, :] = (v - hi.astype(F32)).astype(BF16)

    @pl.loop(0, 4)
    def _(j):
        cols = pl.ds(pl.multiple_of(j * 256, 256), 256)
        acc = jnp.dot(row_lo[...], col_hi[:, cols], preferred_element_type=F32)
        acc += jnp.dot(row_hi[...], col_lo[:, cols], preferred_element_type=F32)
        acc += jnp.dot(row_hi[...], col_hi[:, cols], preferred_element_type=F32)
        for u in range(8):
            tile[2 * u + j // 2, :, pl.ds(pl.multiple_of((j % 2) * 256, 256), 256)] = acc[128 * u : 128 * u + 128]

    mine = pl.ds(pl.multiple_of(k * OWN, OWN), OWN)
    other = pl.ds(pl.multiple_of((1 - k) * OWN, OWN), OWN)

    def dest(dz):
        return lax.rem(z + dz, NZ)

    order = [8]
    for s in range(1, 8):
        order += [8 + s, 8 - s]
    order += [0]
    for i, dz in enumerate(order):
        go(remote(tile.at[dest(dz), other, :], sibling_tile.at[i], s_ssem.at[i], s_rsem.at[i], device(dk=1)))

    def own_sum(dz):
        i = order.index(dz)
        arrived(sibling_tile.at[i], s_rsem.at[i])
        return tile[dest(dz), mine, :] + sibling_tile[i]

    for s in range(8):
        total = own_sum(8 - s)
        if s > 0:
            arrived(up_recv.at[s - 1], up_rsem.at[s - 1])
            total += up_recv[s - 1]
        up_send[s] = total
        go(remote(up_send.at[s], up_recv.at[s], up_ssem.at[s], up_rsem.at[s], device(dz=1)))
        if s < 7:
            total = own_sum(9 + s)
            if s > 0:
                arrived(down_recv.at[s - 1], down_rsem.at[s - 1])
                total += down_recv[s - 1]
            down_send[s] = total
            go(remote(down_send.at[s], down_recv.at[s], down_ssem.at[s], down_rsem.at[s], device(dz=NZ - 1)))

    def rows_of(dy, dk):
        start = lax.rem(y + dy, NY) * QUARTER + lax.rem(k + dk, NK) * OWN
        return pl.ds(pl.multiple_of(start, OWN), OWN)

    here = rows_of(0, 0)
    total = own_sum(0) + earlier_ref[0, here, :]
    arrived(down_recv.at[6], down_rsem.at[6])
    total += down_recv[6]
    arrived(up_recv.at[7], up_rsem.at[7])
    total += up_recv[7]
    out_ref[0, here, :] = total

    for j in (1, 3, 2):
        go(remote(out_ref.at[0, here, :], out_ref.at[0, here, :], o_ssem.at[j], o_rsem.at[4 - j], device(dy=j)))
    for j in (0, 3, 1, 2):
        rows = rows_of(j, 0)
        if j:
            arrived(out_ref.at[0, rows, :], o_rsem.at[j])
        go(remote(out_ref.at[0, rows, :], out_ref.at[0, rows, :], o_ssem.at[4 + j], o_rsem.at[4 + j], device(dk=1)))
    for j in range(4):
        arrived(out_ref.at[0, rows_of(j, 1), :], o_rsem.at[4 + j])
    for copy in sends:
        copy.wait_send()


def body(half_tensor, earlier_blocks):
    vmem = pl.BlockSpec(memory_space=pltpu.VMEM)
    dma = pltpu.SemaphoreType.DMA
    return pl.pallas_call(
        kernel,
        out_shape=jax.ShapeDtypeStruct(earlier_blocks.shape, F32),
        in_specs=[vmem, vmem],
        out_specs=vmem,
        scratch_shapes=[
            pltpu.VMEM((4, PIECE, 128), F32),
            pltpu.VMEM((4, PIECE, 128), F32),
            pltpu.VMEM((8 * PADDED, 128), F32),
            pltpu.VMEM((8 * PADDED, 128), F32),
            pltpu.VMEM((1024, PADDED), BF16),
            pltpu.VMEM((1024, PADDED), BF16),
            pltpu.VMEM((PADDED, 1024), BF16),
            pltpu.VMEM((PADDED, 1024), BF16),
            pltpu.VMEM((NZ, QUARTER, WIDTH), F32),
            pltpu.VMEM((NZ, OWN, WIDTH), F32),
            pltpu.VMEM((8, OWN, WIDTH), F32),
            pltpu.VMEM((7, OWN, WIDTH), F32),
            pltpu.VMEM((8, OWN, WIDTH), F32),
            pltpu.VMEM((7, OWN, WIDTH), F32),
            dma((4, 5)),
            dma((5, 5)),
            dma((4, 5)),
            dma((5, 5)),
            dma((NZ,)),
            dma((NZ,)),
            dma((8,)),
            dma((8,)),
            dma((7,)),
            dma((7,)),
            dma((8,)),
            dma((8,)),
        ],
        compiler_params=pltpu.CompilerParams(
            collective_id=0, has_side_effects=True, vmem_limit_bytes=48 * 2**20
        ),
        cost_estimate=pl.CostEstimate(
            flops=6 * 1024 * 1024 * DEPTH, bytes_accessed=3 * 2**20, transcendentals=0
        ),
    )(half_tensor, earlier_blocks)


def solution(mesh):
    return jax.shard_map(
        body,
        mesh=mesh,
        in_specs=(P("row", "col", None), P("row", None, None)),
        out_specs=P("row", None, None),
        check_vma=False,
    )
```

time: 725 us -> 111 us (0.15)
  waiting for transfers between devices: 345 us -> 0 us
  blocking collectives: 302 us -> 0 us
  Pallas kernels: 0 us -> 108 us
  local copies, waits for them, and re-layouts: 22.2 us -> 2.69 us
  starting transfers between devices: 19.4 us -> 0 us
  matrix products: 16.4 us -> 0 us
  between operations: 13.4 us -> 0.02 us
    all_to_all x1 -> x0, blocking collectives: 302 us -> none  [body(): lax.all_to_all(second_groups, 'row', split_axis=2, concat_axis=0, tiled=T...]
    all_to_all x1 -> x0, waiting for transfers between devices: 274 us -> none  [body(): lax.all_to_all(first_groups, 'row', split_axis=2, concat_axis=0, tiled=True)]
    pallas_call x0 -> x1, Pallas kernels: none -> 108 us  [body(): pl.pallas_call(kernel, out_shape=jax.ShapeDtypeStruct(earlier_blocks.shap...]
    psum x1 -> x0, waiting for transfers between devices: 71.2 us -> none  [body(): summed = lax.psum(partial_block, 'col')]
    broadcast_in_dim x4 -> x0, local copies, waits for them, and re-layouts: 21.7 us -> none  [the longest x3 12.4 us: body(): jnp.broadcast_to(half_tensor.reshape(aux_dev, occ_dev, grid_side, 1, widt...]
    all_to_all x1 -> x0, starting transfers between devices: 19.3 us -> none  [body(): lax.all_to_all(first_groups, 'row', split_axis=2, concat_axis=0, tiled=True)]
    dot_general x1 -> x0, matrix products: 16.4 us -> none  [body(): jnp.einsum('pom,poxn->mn', row_whole, lax.all_to_all(second_groups, 'row'...]
  transfers between devices with their start and end apart: 2 -> 0, of which waited for: 2 -> 0; matrix products, arithmetic and copies ran while one was open for 1% -> 0% of each run, Pallas kernels for 0% -> 0%
where the time goes in v1:
time: 111 us
  Pallas kernels  108 us (97%)
  local copies, waits for them, and re-layouts  2.69 us (2%)
    pallas_call x1, Pallas kernels, body(): pl.pallas_call(kernel, out_shape=jax.ShapeDtypeStruct(earlier_blocks.shap...  108 us
    unnamed x4, local copies, waits for them, and re-layouts  2.69 us

profile of v1, /device:TPU:1, one launch (start us, length us, event | category | flops | bytes accessed | tf_op | source)
XLA Modules:
  0.0 110.7 jit_solution(5604085421316689453)
XLA Ops:
  0.0 0.0 copy-start
  0.0 1.7 %copy.3.half_ref = f32[1,50,4096]{2,1,0:T(8,128)S(1)} copy(f32[1,50,4096]{2,0,1:T(1,128)} %param.2) | data formatting | bytes 1638400 | tf_op args[0]
  1.7 0.0 copy-done
  1.7 108.0 %shard_map.28 = f32[1,512,512]{2,1,0:T(8,128)S(1)} custom-call(f32[1,50,4096]{2,1,0:T(8,128)S(1)} %copy.3.half_ref, f32[1,512,512]{2,1,0:T(8,128)S(1)} %copy-done), custom_call_target="tpu_custom_call" | custom-call | flops 5033164800 | bytes 3145728 | tf_op jit(solution)/shard_map/pallas_call | solution.py:220
  109.7 1.0 copy.5
Async XLA Ops:
  0.0 1.7 %copy-start = (f32[1,512,512]{2,1,0:T(8,128)S(1)}, f32[1,512,512]{2,1,0:T(8,128)}, u32[]{:S(2)}) copy-start(f32[1,512,512]{2,1,0:T(8,128)} %earlier_ref.1) | copy-start | bytes 3145732

commit v2 on v1

v2 whole, which is shorter than its diff:
```python
import jax
import jax.numpy as jnp
from jax import lax
from jax.experimental import pallas as pl
from jax.experimental.pallas import tpu as pltpu
from jax.sharding import PartitionSpec as P

MESH = pl.DeviceIdType.MESH
F32 = jnp.float32
BF16 = jnp.bfloat16

NX, NY, NZ, NK = 4, 4, 16, 2
ROWS = 50
PIECE = ROWS * 8
HALF = 25 * 8
DEPTH = 256
QUARTER = 128
OWN = 64
CHUNKS = 2
PART = OWN // CHUNKS
WIDTH = 512

GROUPS = (
    ((0, 0), (0, 3), (3, 0), (3, 3)),
    ((0, 1), (1, 0), (1, 1), (1, 3), (3, 1)),
    ((0, 2), (2, 0), (3, 2), (2, 3)),
    ((1, 2), (2, 1), (2, 2)),
)
PLACE = {source: (g, i) for g, group in enumerate(GROUPS) for i, source in enumerate(group)}
OFFSETS = (4, 3, 5, 2, 6, 1, 7, 0)


def kernel(
    half_hbm,
    earlier_hbm,
    out_ref,
    half,
    earlier,
    col_send,
    row_send,
    col_buf,
    row_buf,
    row_hi,
    row_lo,
    col_hi,
    col_lo,
    tile,
    sibling_tile,
    up_send,
    down_send,
    up_recv,
    down_recv,
    in_sem,
    c_ssem,
    c_rsem,
    r_ssem,
    r_rsem,
    s_ssem,
    s_rsem,
    up_ssem,
    up_rsem,
    down_ssem,
    down_rsem,
    o_ssem,
    o_rsem,
):
    r = lax.axis_index("row")
    c = lax.axis_index("col")
    z, x, y, k = r // NX, r % NX, c // NK, c % NK
    odd = z % 2

    def device(dz=0, dx=0, dy=0, dk=0):
        return (
            lax.rem(z + dz, NZ) * NX + lax.rem(x + dx, NX),
            lax.rem(y + dy, NY) * NK + lax.rem(k + dk, NK),
        )

    def remote(src, dst, ssem, rsem, to):
        return pltpu.make_async_remote_copy(
            src_ref=src, dst_ref=dst, send_sem=ssem, recv_sem=rsem, device_id=to, device_id_type=MESH
        )

    def rows_of(dy, dk, chunk=None):
        start = lax.rem(y + dy, NY) * QUARTER + lax.rem(k + dk, NK) * OWN
        if chunk is None:
            return pl.ds(pl.multiple_of(start, OWN), OWN)
        return pl.ds(pl.multiple_of(start + chunk * PART, PART), PART)

    load = pltpu.make_async_copy(half_hbm, half, in_sem.at[0])
    load.start()
    load_earlier = pltpu.make_async_copy(earlier_hbm.at[0, rows_of(0, 0), :], earlier, in_sem.at[1])
    load_earlier.start()

    peers = [device(dx=j) for j in range(1, NX)] + [device(dy=j) for j in range(1, NY)]
    peers += [device(dz=1), device(dz=NZ - 1), device(dk=1)]
    barrier = pltpu.get_barrier_semaphore()
    for peer in peers:
        pl.semaphore_signal(barrier, inc=1, device_id=peer, device_id_type=MESH)

    def slot(buf, dx, dy, part=None):
        group, i = PLACE[dx, dy]
        if part is None:
            return buf.at[group, pl.ds(i * PIECE, PIECE), :]
        return buf.at[group, pl.ds(i * PIECE + part * HALF, HALF), :]

    for g, group in enumerate(GROUPS):
        filled = len(group) * PIECE
        pad = jnp.zeros((8 * DEPTH - filled, 128), F32)
        col_buf[g, pl.ds(filled, 8 * DEPTH - filled), :] = pad
        row_buf[g, pl.ds(filled, 8 * DEPTH - filled), :] = pad

    load.wait()
    for i in range(ROWS):
        for n in range(4):
            low = half[pl.ds(32 * i + 4 * n, 4), :]
            high = half[pl.ds(32 * i + 16 + 4 * n, 4), :]
            col_send[n, pl.ds(8 * i, 4), :] = low
            col_send[n, pl.ds(8 * i + 4, 4), :] = high
            row_send[n, pl.ds(8 * i, 8), :] = half[pl.ds(32 * i + n, 8, stride=4), :]

    pl.semaphore_wait(barrier, len(peers))

    sends = []

    def go(copy):
        copy.start()
        sends.append(copy)

    for j in (1, 3, 2):
        go(remote(col_send.at[lax.rem(x + j, NX)], slot(col_buf, 4 - j, 0), c_ssem.at[j, 0], c_rsem.at[4 - j, 0], device(dx=j)))
        go(remote(row_send.at[lax.rem(y + j, NY)], slot(row_buf, 0, 4 - j), r_ssem.at[j, 0], r_rsem.at[0, 4 - j], device(dy=j)))
    slot(col_buf, 0, 0)[...] = col_send[x]
    slot(row_buf, 0, 0)[...] = row_send[y]

    def spread(a):
        go(remote(slot(col_buf, a, 0), slot(col_buf, a, 3), c_ssem.at[a, 1], c_rsem.at[a, 3], device(dy=1)))
        go(remote(slot(row_buf, 0, a), slot(row_buf, 3, a), r_ssem.at[a, 1], r_rsem.at[3, a], device(dx=1)))
        go(remote(slot(col_buf, a, 0), slot(col_buf, a, 1), c_ssem.at[a, 2], c_rsem.at[a, 1], device(dy=3)))
        go(remote(slot(row_buf, 0, a), slot(row_buf, 1, a), r_ssem.at[a, 2], r_rsem.at[1, a], device(dx=3)))

    def arrived(dst, rsem):
        remote(dst, dst, rsem, rsem, device(dy=1)).wait_recv()

    def forward(a):
        arrived(slot(col_buf, a, 3), c_rsem.at[a, 3])
        go(remote(slot(col_buf, a, 3, 0), slot(col_buf, a, 2, 0), c_ssem.at[a, 3], c_rsem.at[a, 2], device(dy=1)))
        arrived(slot(row_buf, 3, a), r_rsem.at[3, a])
        go(remote(slot(row_buf, 3, a, 0), slot(row_buf, 2, a, 0), r_ssem.at[a, 3], r_rsem.at[2, a], device(dx=1)))
        arrived(slot(col_buf, a, 1), c_rsem.at[a, 1])
        go(remote(slot(col_buf, a, 1, 1), slot(col_buf, a, 2, 1), c_ssem.at[a, 4], c_rsem.at[a, 4], device(dy=3)))
        arrived(slot(row_buf, 1, a), r_rsem.at[1, a])
        go(remote(slot(row_buf, 1, a, 1), slot(row_buf, 2, a, 1), r_ssem.at[a, 4], r_rsem.at[4, a], device(dx=3)))

    def finish(a):
        arrived(slot(col_buf, a, 2, 0), c_rsem.at[a, 2])
        arrived(slot(row_buf, 2, a, 0), r_rsem.at[2, a])
        arrived(slot(col_buf, a, 2, 1), c_rsem.at[a, 4])
        arrived(slot(row_buf, 2, a, 1), r_rsem.at[4, a])

    def split(g):
        for n in range(8):
            v = col_buf[g, pl.ds(n, DEPTH, stride=8), :]
            hi = v.astype(BF16)
            col_hi[:, 128 * n : 128 * n + 128] = hi
            col_lo[:, 128 * n : 128 * n + 128] = (v - hi.astype(F32)).astype(BF16)
            offset = odd * ((8 - OFFSETS[n]) % 8) + (1 - odd) * OFFSETS[n]
            u = lax.rem(z // 2 + offset, 8)
            v = row_buf[g, pl.ds(u, DEPTH, stride=8), :].T
            hi = v.astype(BF16)
            row_hi[128 * n : 128 * n + 128, :] = hi
            row_lo[128 * n : 128 * n + 128, :] = (v - hi.astype(F32)).astype(BF16)

    def product(rows, cols):
        acc = jnp.dot(row_lo[rows, :], col_hi[:, cols], preferred_element_type=F32)
        acc += jnp.dot(row_hi[rows, :], col_lo[:, cols], preferred_element_type=F32)
        acc += jnp.dot(row_hi[rows, :], col_hi[:, cols], preferred_element_type=F32)
        return acc

    def multiply(g):
        split(g)

        @pl.loop(0, 4)
        def _(j):
            acc = product(slice(None), pl.ds(pl.multiple_of(j * 256, 256), 256))
            cols = pl.ds(pl.multiple_of((j % 2) * 256, 256), 256)
            for n in range(8):
                part = acc[128 * n : 128 * n + 128]
                if g > 0:
                    part += tile[2 * n + j // 2, :, cols]
                tile[2 * n + j // 2, :, cols] = part

    spread(0)
    for a in (3, 1, 2):
        arrived(slot(col_buf, a, 0), c_rsem.at[a, 0])
        arrived(slot(row_buf, 0, a), r_rsem.at[0, a])
        spread(a)
        if a == 3:
            forward(0)
    forward(3)
    multiply(0)
    forward(1)
    multiply(1)
    forward(2)
    finish(0)
    finish(3)
    multiply(2)
    finish(1)
    finish(2)
    split(3)

    other = pl.ds(pl.multiple_of((1 - k) * OWN, OWN), OWN)

    def last(m):
        for j in range(4):
            acc = product(slice(256 * m, 256 * m + 256), slice(256 * j, 256 * j + 256))
            cols = slice((j % 2) * 256, (j % 2) * 256 + 256)
            for n in range(2):
                tile[4 * m + 2 * n + j // 2, :, cols] += acc[128 * n : 128 * n + 128]
        for n in (2 * m, 2 * m + 1):
            go(remote(tile.at[pl.ds(2 * n, 2), other, :], sibling_tile.at[pl.ds(2 * n, 2)], s_ssem.at[n], s_rsem.at[n], device(dk=1)))

    def sibling_arrived(n):
        arrived(sibling_tile.at[pl.ds(2 * n, 2)], s_rsem.at[n])

    def own_sum(dz, chunk):
        def index(distance, flip):
            n = OFFSETS.index(distance // 2)
            return 2 * n + (distance % 2 if not flip else 1 - distance % 2)

        i = odd * index((NZ - dz) % NZ, True) + (1 - odd) * index(dz, False)
        mine = pl.ds(pl.multiple_of(k * OWN + chunk * PART, PART), PART)
        return tile[i, mine, :] + sibling_tile[i, pl.ds(chunk * PART, PART), :]

    def step(s):
        for ch in range(CHUNKS):
            total = own_sum(8 - s, ch)
            if s > 0:
                arrived(up_recv.at[s - 1, ch], up_rsem.at[s - 1, ch])
                total += up_recv[s - 1, ch]
            up_send[s, ch] = total
            go(remote(up_send.at[s, ch], up_recv.at[s, ch], up_ssem.at[s, ch], up_rsem.at[s, ch], device(dz=1)))
            if s < 7:
                total = own_sum(9 + s, ch)
                if s > 0:
                    arrived(down_recv.at[s - 1, ch], down_rsem.at[s - 1, ch])
                    total += down_recv[s - 1, ch]
                down_send[s, ch] = total
                go(remote(down_send.at[s, ch], down_recv.at[s, ch], down_ssem.at[s, ch], down_rsem.at[s, ch], device(dz=NZ - 1)))

    last(0)
    last(1)
    sibling_arrived(0)
    sibling_arrived(1)
    step(0)
    last(2)
    sibling_arrived(2)
    step(1)
    last(3)
    sibling_arrived(3)
    step(2)
    for s in range(3, 8):
        if s < 7:
            sibling_arrived(s + 1)
        step(s)

    load_earlier.wait()
    for ch in range(CHUNKS):
        here = rows_of(0, 0, ch)
        total = own_sum(0, ch) + earlier[pl.ds(ch * PART, PART), :]
        arrived(down_recv.at[6, ch], down_rsem.at[6, ch])
        total += down_recv[6, ch]
        arrived(up_recv.at[7, ch], up_rsem.at[7, ch])
        total += up_recv[7, ch]
        out_ref[0, here, :] = total
        for j in (1, 3, 2):
            go(remote(out_ref.at[0, here, :], out_ref.at[0, here, :], o_ssem.at[j, ch], o_rsem.at[4 - j, ch], device(dy=j)))
        go(remote(out_ref.at[0, here, :], out_ref.at[0, here, :], o_ssem.at[4, ch], o_rsem.at[4, ch], device(dk=1)))
    for ch in range(CHUNKS):
        for j in (3, 1, 2):
            rows = rows_of(j, 0, ch)
            arrived(out_ref.at[0, rows, :], o_rsem.at[j, ch])
            go(remote(out_ref.at[0, rows, :], out_ref.at[0, rows, :], o_ssem.at[4 + j, ch], o_rsem.at[4 + j, ch], device(dk=1)))
    for ch in range(CHUNKS):
        for j in range(4):
            arrived(out_ref.at[0, rows_of(j, 1, ch), :], o_rsem.at[4 + j, ch])
    for copy in sends:
        copy.wait_send()


def body(half_tensor, earlier_blocks):
    vmem = pl.BlockSpec(memory_space=pltpu.VMEM)
    hbm = pl.BlockSpec(memory_space=pl.ANY)
    dma = pltpu.SemaphoreType.DMA
    return pl.pallas_call(
        kernel,
        out_shape=jax.ShapeDtypeStruct(earlier_blocks.shape, F32),
        in_specs=[hbm, hbm],
        out_specs=vmem,
        scratch_shapes=[
            pltpu.VMEM((ROWS * 32, 128), F32),
            pltpu.VMEM((OWN, WIDTH), F32),
            pltpu.VMEM((4, PIECE, 128), F32),
            pltpu.VMEM((4, PIECE, 128), F32),
            pltpu.VMEM((4, 8 * DEPTH, 128), F32),
            pltpu.VMEM((4, 8 * DEPTH, 128), F32),
            pltpu.VMEM((1024, DEPTH), BF16),
            pltpu.VMEM((1024, DEPTH), BF16),
            pltpu.VMEM((DEPTH, 1024), BF16),
            pltpu.VMEM((DEPTH, 1024), BF16),
            pltpu.VMEM((NZ, QUARTER, WIDTH), F32),
            pltpu.VMEM((NZ, OWN, WIDTH), F32),
            pltpu.VMEM((8, CHUNKS, PART, WIDTH), F32),
            pltpu.VMEM((7, CHUNKS, PART, WIDTH), F32),
            pltpu.VMEM((8, CHUNKS, PART, WIDTH), F32),
            pltpu.VMEM((7, CHUNKS, PART, WIDTH), F32),
            dma((2,)),
            dma((4, 5)),
            dma((4, 5)),
            dma((4, 5)),
            dma((5, 5)),
            dma((8,)),
            dma((8,)),
            dma((8, CHUNKS)),
            dma((8, CHUNKS)),
            dma((7, CHUNKS)),
            dma((7, CHUNKS)),
            dma((8, CHUNKS)),
            dma((8, CHUNKS)),
        ],
        compiler_params=pltpu.CompilerParams(
            collective_id=0, has_side_effects=True, vmem_limit_bytes=48 * 2**20
        ),
        cost_estimate=pl.CostEstimate(
            flops=6 * 1024 * 1024 * 16 * ROWS, bytes_accessed=3 * 2**20, transcendentals=0
        ),
    )(half_tensor.reshape(ROWS * 32, 128), earlier_blocks)


def solution(mesh):
    return jax.shard_map(
        body,
        mesh=mesh,
        in_specs=(P("row", "col", None), P("row", None, None)),
        out_specs=P("row", None, None),
        check_vma=False,
    )
```

time: 111 us -> 95.9 us (0.86)
  Pallas kernels: 108 us -> 92.3 us
    pallas_call x1, Pallas kernels: 108 us -> 92.3 us  [body(): pl.pallas_call(kernel, out_shape=jax.ShapeDtypeStruct(earlier_blocks.shap...]
    unnamed x4 -> x5, local copies, waits for them, and re-layouts: 2.69 us -> 3.34 us
where the time goes in v2:
time: 95.9 us; the launch traced here: 95.7 us
  Pallas kernels  92.3 us (96%)
  local copies, waits for them, and re-layouts  3.34 us (3%)
    pallas_call x1, Pallas kernels, body(): pl.pallas_call(kernel, out_shape=jax.ShapeDtypeStruct(earlier_blocks.shap...  92.3 us
    unnamed x5, local copies, waits for them, and re-layouts  3.34 us

profile of v2, /device:TPU:1, one launch (start us, length us, event | category | flops | bytes accessed | tf_op | source)
XLA Modules:
  0.0 95.7 jit_solution(1043858631486000063)
XLA Ops:
  0.0 0.0 copy-start
  0.0 1.2 %copy-done = f32[1,512,512]{2,1,0:T(8,128)S(1)} copy-done((f32[1,512,512]{2,1,0:T(8,128)S(1)}, f32[1,512,512]{2,1,0:T(8,128)}, u32[]{:S(2)}) %copy-start) | copy-done | bytes 1048600
  1.2 0.0 copy-start.1
  1.2 1.1 %copy-done.1 = f32[1,50,4096]{2,0,1:T(1,128)S(1)} copy-done((f32[1,50,4096]{2,0,1:T(1,128)S(1)}, f32[1,50,4096]{2,0,1:T(1,128)}, u32[]{:S(2)}) %copy-start.1) | copy-done | bytes 819224
  2.4 92.3 %shard_map.28 = f32[1,512,512]{2,1,0:T(8,128)S(1)} custom-call(f32[1600,128]{1,0:T(8,128)S(1)} %bitcast.1, f32[1,512,512]{2,1,0:T(8,128)S(1)} %copy-done), custom_call_target="tpu_custom_call" | custom-call | flops 5033164800 | bytes 3145728 | tf_op jit(solution)/shard_map/pallas_call | solution.py:294
  94.7 1.0 %copy.4 = f32[1,512,512]{2,1,0:T(8,128)} copy(f32[1,512,512]{2,1,0:T(8,128)S(1)} %shard_map.28) | data formatting | bytes 2097152
Async XLA Ops:
  0.0 1.2 %copy-start = (f32[1,512,512]{2,1,0:T(8,128)S(1)}, f32[1,512,512]{2,1,0:T(8,128)}, u32[]{:S(2)}) copy-start(f32[1,512,512]{2,1,0:T(8,128)} %earlier_hbm.1) | copy-start | bytes 3145732
  1.2 1.1 %copy-start.1 = (f32[1,50,4096]{2,0,1:T(1,128)S(1)}, f32[1,50,4096]{2,0,1:T(1,128)}, u32[]{:S(2)}) copy-start(f32[1,50,4096]{2,0,1:T(1,128)} %param.2) | copy-start | bytes 2457604

commit v3 on v2

--- a/solution.py
+++ b/solution.py
@@ -16,8 +16,9 @@
 DEPTH = 256
 QUARTER = 128
 OWN = 64
-CHUNKS = 2
+CHUNKS = 4
 PART = OWN // CHUNKS
+HALVED = (2,)
 WIDTH = 512
 
 GROUPS = (
@@ -31,10 +32,9 @@
 
 
 def kernel(
-    half_hbm,
+    half,
     earlier_hbm,
     out_ref,
-    half,
     earlier,
     col_send,
     row_send,
@@ -46,10 +46,8 @@
     col_lo,
     tile,
     sibling_tile,
-    up_send,
-    down_send,
-    up_recv,
-    down_recv,
+    ring_send,
+    ring_recv,
     in_sem,
     c_ssem,
     c_rsem,
@@ -57,10 +55,8 @@
     r_rsem,
     s_ssem,
     s_rsem,
-    up_ssem,
-    up_rsem,
-    down_ssem,
-    down_rsem,
+    ring_ssem,
+    ring_rsem,
     o_ssem,
     o_rsem,
 ):
@@ -86,9 +82,7 @@
             return pl.ds(pl.multiple_of(start, OWN), OWN)
         return pl.ds(pl.multiple_of(start + chunk * PART, PART), PART)
 
-    load = pltpu.make_async_copy(half_hbm, half, in_sem.at[0])
-    load.start()
-    load_earlier = pltpu.make_async_copy(earlier_hbm.at[0, rows_of(0, 0), :], earlier, in_sem.at[1])
+    load_earlier = pltpu.make_async_copy(earlier_hbm.at[0, rows_of(0, 0), :], earlier, in_sem.at[0])
     load_earlier.start()
 
     peers = [device(dx=j) for j in range(1, NX)] + [device(dy=j) for j in range(1, NY)]
@@ -103,21 +97,15 @@
             return buf.at[group, pl.ds(i * PIECE, PIECE), :]
         return buf.at[group, pl.ds(i * PIECE + part * HALF, HALF), :]
 
-    for g, group in enumerate(GROUPS):
-        filled = len(group) * PIECE
-        pad = jnp.zeros((8 * DEPTH - filled, 128), F32)
-        col_buf[g, pl.ds(filled, 8 * DEPTH - filled), :] = pad
-        row_buf[g, pl.ds(filled, 8 * DEPTH - filled), :] = pad
-
-    load.wait()
-    for i in range(ROWS):
-        for n in range(4):
-            low = half[pl.ds(32 * i + 4 * n, 4), :]
-            high = half[pl.ds(32 * i + 16 + 4 * n, 4), :]
-            col_send[n, pl.ds(8 * i, 4), :] = low
-            col_send[n, pl.ds(8 * i + 4, 4), :] = high
-            row_send[n, pl.ds(8 * i, 8), :] = half[pl.ds(32 * i + n, 8, stride=4), :]
-
+    def prepare(j):
+        n = lax.rem(x + j, NX)
+        m = lax.rem(y + j, NY)
+        for i in range(ROWS):
+            col_send[j, pl.ds(8 * i, 4), :] = half[pl.ds(32 * i + 4 * n, 4), :]
+            col_send[j, pl.ds(8 * i + 4, 4), :] = half[pl.ds(32 * i + 16 + 4 * n, 4), :]
+            row_send[j, pl.ds(8 * i, 8), :] = half[pl.ds(32 * i + m, 8, stride=4), :]
+
+    prepare(1)
     pl.semaphore_wait(barrier, len(peers))
 
     sends = []
@@ -127,29 +115,42 @@
         sends.append(copy)
 
     for j in (1, 3, 2):
-        go(remote(col_send.at[lax.rem(x + j, NX)], slot(col_buf, 4 - j, 0), c_ssem.at[j, 0], c_rsem.at[4 - j, 0], device(dx=j)))
-        go(remote(row_send.at[lax.rem(y + j, NY)], slot(row_buf, 0, 4 - j), r_ssem.at[j, 0], r_rsem.at[0, 4 - j], device(dy=j)))
-    slot(col_buf, 0, 0)[...] = col_send[x]
-    slot(row_buf, 0, 0)[...] = row_send[y]
+        if j != 1:
+            prepare(j)
+        go(remote(col_send.at[j], slot(col_buf, 4 - j, 0), c_ssem.at[j, 0], c_rsem.at[4 - j, 0], device(dx=j)))
+        go(remote(row_send.at[j], slot(row_buf, 0, 4 - j), r_ssem.at[j, 0], r_rsem.at[0, 4 - j], device(dy=j)))
+    prepare(0)
+    slot(col_buf, 0, 0)[...] = col_send[0]
+    slot(row_buf, 0, 0)[...] = row_send[0]
 
     def spread(a):
-        go(remote(slot(col_buf, a, 0), slot(col_buf, a, 3), c_ssem.at[a, 1], c_rsem.at[a, 3], device(dy=1)))
-        go(remote(slot(row_buf, 0, a), slot(row_buf, 3, a), r_ssem.at[a, 1], r_rsem.at[3, a], device(dx=1)))
-        go(remote(slot(col_buf, a, 0), slot(col_buf, a, 1), c_ssem.at[a, 2], c_rsem.at[a, 1], device(dy=3)))
-        go(remote(slot(row_buf, 0, a), slot(row_buf, 1, a), r_ssem.at[a, 2], r_rsem.at[1, a], device(dx=3)))
+        for part, up, down in ((0, 1, 2), (1, 5, 6)) if a in HALVED else ((None, 1, 2),):
+            other = None if part is None else 1 - part
+            up_to = 3 if up == 1 else 5
+            down_to = 1 if down == 2 else 6
+            go(remote(slot(col_buf, a, 0, part), slot(col_buf, a, 3, part), c_ssem.at[a, up], c_rsem.at[a, up_to], device(dy=1)))
+            go(remote(slot(row_buf, 0, a, part), slot(row_buf, 3, a, part), r_ssem.at[a, up], r_rsem.at[up_to, a], device(dx=1)))
+            go(remote(slot(col_buf, a, 0, other), slot(col_buf, a, 1, other), c_ssem.at[a, down], c_rsem.at[a, down_to], device(dy=3)))
+            go(remote(slot(row_buf, 0, a, other), slot(row_buf, 1, a, other), r_ssem.at[a, down], r_rsem.at[down_to, a], device(dx=3)))
 
     def arrived(dst, rsem):
         remote(dst, dst, rsem, rsem, device(dy=1)).wait_recv()
 
     def forward(a):
-        arrived(slot(col_buf, a, 3), c_rsem.at[a, 3])
+        low, high = (0, 1) if a in HALVED else (None, None)
+        arrived(slot(col_buf, a, 3, low), c_rsem.at[a, 3])
         go(remote(slot(col_buf, a, 3, 0), slot(col_buf, a, 2, 0), c_ssem.at[a, 3], c_rsem.at[a, 2], device(dy=1)))
-        arrived(slot(row_buf, 3, a), r_rsem.at[3, a])
+        arrived(slot(row_buf, 3, a, low), r_rsem.at[3, a])
         go(remote(slot(row_buf, 3, a, 0), slot(row_buf, 2, a, 0), r_ssem.at[a, 3], r_rsem.at[2, a], device(dx=1)))
-        arrived(slot(col_buf, a, 1), c_rsem.at[a, 1])
+        arrived(slot(col_buf, a, 1, high), c_rsem.at[a, 1])
         go(remote(slot(col_buf, a, 1, 1), slot(col_buf, a, 2, 1), c_ssem.at[a, 4], c_rsem.at[a, 4], device(dy=3)))
-        arrived(slot(row_buf, 1, a), r_rsem.at[1, a])
+        arrived(slot(row_buf, 1, a, high), r_rsem.at[1, a])
         go(remote(slot(row_buf, 1, a, 1), slot(row_buf, 2, a, 1), r_ssem.at[a, 4], r_rsem.at[4, a], device(dx=3)))
+        if a in HALVED:
+            arrived(slot(col_buf, a, 3, 1), c_rsem.at[a, 5])
+            arrived(slot(row_buf, 3, a, 1), r_rsem.at[5, a])
+            arrived(slot(col_buf, a, 1, 0), c_rsem.at[a, 6])
+            arrived(slot(row_buf, 1, a, 0), r_rsem.at[6, a])
 
     def finish(a):
         arrived(slot(col_buf, a, 2, 0), c_rsem.at[a, 2])
@@ -190,6 +191,11 @@
                 tile[2 * n + j // 2, :, cols] = part
 
     spread(0)
+    for g, group in enumerate(GROUPS):
+        filled = len(group) * PIECE
+        pad = jnp.zeros((8 * DEPTH - filled, 128), F32)
+        col_buf[g, pl.ds(filled, 8 * DEPTH - filled), :] = pad
+        row_buf[g, pl.ds(filled, 8 * DEPTH - filled), :] = pad
     for a in (3, 1, 2):
         arrived(slot(col_buf, a, 0), c_rsem.at[a, 0])
         arrived(slot(row_buf, 0, a), r_rsem.at[0, a])
@@ -222,30 +228,27 @@
     def sibling_arrived(n):
         arrived(sibling_tile.at[pl.ds(2 * n, 2)], s_rsem.at[n])
 
-    def own_sum(dz, chunk):
-        def index(distance, flip):
-            n = OFFSETS.index(distance // 2)
-            return 2 * n + (distance % 2 if not flip else 1 - distance % 2)
-
-        i = odd * index((NZ - dz) % NZ, True) + (1 - odd) * index(dz, False)
+    def own_sum(way, distance, chunk):
+        def slot_of(dz):
+            n = 2 * OFFSETS.index(dz // 2) + dz % 2
+            return (1 - odd) * n + odd * (n + 1 - 2 * (n % 2))
+
+        side = (way + k + odd) % 2
+        n = (1 - side) * slot_of(distance) + side * slot_of((NZ - distance) % NZ)
         mine = pl.ds(pl.multiple_of(k * OWN + chunk * PART, PART), PART)
-        return tile[i, mine, :] + sibling_tile[i, pl.ds(chunk * PART, PART), :]
+        return tile[n, mine, :] + sibling_tile[n, pl.ds(chunk * PART, PART), :]
 
     def step(s):
-        for ch in range(CHUNKS):
-            total = own_sum(8 - s, ch)
-            if s > 0:
-                arrived(up_recv.at[s - 1, ch], up_rsem.at[s - 1, ch])
-                total += up_recv[s - 1, ch]
-            up_send[s, ch] = total
-            go(remote(up_send.at[s, ch], up_recv.at[s, ch], up_ssem.at[s, ch], up_rsem.at[s, ch], device(dz=1)))
-            if s < 7:
-                total = own_sum(9 + s, ch)
-                if s > 0:
-                    arrived(down_recv.at[s - 1, ch], down_rsem.at[s - 1, ch])
-                    total += down_recv[s - 1, ch]
-                down_send[s, ch] = total
-                go(remote(down_send.at[s, ch], down_recv.at[s, ch], down_ssem.at[s, ch], down_rsem.at[s, ch], device(dz=NZ - 1)))
+        for i in range(2, CHUNKS) if s == 0 else range(CHUNKS):
+            for way in range(2):
+                ch = (i + 2 * (1 - way)) % CHUNKS
+                total = own_sum(way, 8 - s, ch)
+                if s > 1 or (s == 1 and i > 1):
+                    arrived(ring_recv.at[way, s - 1, ch], ring_rsem.at[way, s - 1, ch])
+                    total += ring_recv[way, s - 1, ch]
+                ring_send[way, s, ch] = total
+                to = device(dz=1 + 14 * ((way + k) % 2))
+                go(remote(ring_send.at[way, s, ch], ring_recv.at[way, s, ch], ring_ssem.at[way, s, ch], ring_rsem.at[way, s, ch], to))
 
     last(0)
     last(1)
@@ -265,14 +268,13 @@
 
     load_earlier.wait()
     for ch in range(CHUNKS):
+        total = own_sum(0, 0, ch) + earlier[pl.ds(ch * PART, PART), :]
+        for way in range(2):
+            arrived(ring_recv.at[way, 7, ch], ring_rsem.at[way, 7, ch])
+            total += ring_recv[way, 7, ch]
         here = rows_of(0, 0, ch)
-        total = own_sum(0, ch) + earlier[pl.ds(ch * PART, PART), :]
-        arrived(down_recv.at[6, ch], down_rsem.at[6, ch])
-        total += down_recv[6, ch]
-        arrived(up_recv.at[7, ch], up_rsem.at[7, ch])
-        total += up_recv[7, ch]
         out_ref[0, here, :] = total
-        for j in (1, 3, 2):
+        for j in (2, 1, 3):
             go(remote(out_ref.at[0, here, :], out_ref.at[0, here, :], o_ssem.at[j, ch], o_rsem.at[4 - j, ch], device(dy=j)))
         go(remote(out_ref.at[0, here, :], out_ref.at[0, here, :], o_ssem.at[4, ch], o_rsem.at[4, ch], device(dk=1)))
     for ch in range(CHUNKS):
@@ -294,10 +296,9 @@
     return pl.pallas_call(
         kernel,
         out_shape=jax.ShapeDtypeStruct(earlier_blocks.shape, F32),
-        in_specs=[hbm, hbm],
+        in_specs=[vmem, hbm],
         out_specs=vmem,
         scratch_shapes=[
-            pltpu.VMEM((ROWS * 32, 128), F32),
             pltpu.VMEM((OWN, WIDTH), F32),
             pltpu.VMEM((4, PIECE, 128), F32),
             pltpu.VMEM((4, PIECE, 128), F32),
@@ -309,26 +310,22 @@
             pltpu.VMEM((DEPTH, 1024), BF16),
             pltpu.VMEM((NZ, QUARTER, WIDTH), F32),
             pltpu.VMEM((NZ, OWN, WIDTH), F32),
-            pltpu.VMEM((8, CHUNKS, PART, WIDTH), F32),
-            pltpu.VMEM((7, CHUNKS, PART, WIDTH), F32),
-            pltpu.VMEM((8, CHUNKS, PART, WIDTH), F32),
-            pltpu.VMEM((7, CHUNKS, PART, WIDTH), F32),
-            dma((2,)),
-            dma((4, 5)),
-            dma((4, 5)),
-            dma((4, 5)),
-            dma((5, 5)),
+            pltpu.VMEM((2, 8, CHUNKS, PART, WIDTH), F32),
+            pltpu.VMEM((2, 8, CHUNKS, PART, WIDTH), F32),
+            dma((1,)),
+            dma((4, 7)),
+            dma((4, 7)),
+            dma((4, 7)),
+            dma((7, 5)),
             dma((8,)),
             dma((8,)),
-            dma((8, CHUNKS)),
-            dma((8, CHUNKS)),
-            dma((7, CHUNKS)),
-            dma((7, CHUNKS)),
+            dma((2, 8, CHUNKS)),
+            dma((2, 8, CHUNKS)),
             dma((8, CHUNKS)),
             dma((8, CHUNKS)),
         ],
         compiler_params=pltpu.CompilerParams(
-            collective_id=0, has_side_effects=True, vmem_limit_bytes=48 * 2**20
+            collective_id=0, has_side_effects=True, vmem_limit_bytes=52 * 2**20
         ),
         cost_estimate=pl.CostEstimate(
             flops=6 * 1024 * 1024 * 16 * ROWS, bytes_accessed=3 * 2**20, transcendentals=0

time: 95.9 us -> 91.9 us (0.958)
  Pallas kernels: 92.3 us -> 89.7 us
  local copies, waits for them, and re-layouts: 3.34 us -> 2.12 us
    pallas_call x1, Pallas kernels: 92.3 us -> 89.7 us  [body(): pl.pallas_call(kernel, out_shape=jax.ShapeDtypeStruct(earlier_blocks.shap...]
    unnamed x5 -> x3, local copies, waits for them, and re-layouts: 3.34 us -> 2.12 us
where the time goes in v3:
time: 91.9 us; the launch traced here: 91.8 us
  Pallas kernels  89.7 us (98%)
  local copies, waits for them, and re-layouts  2.12 us (2%)
    pallas_call x1, Pallas kernels, body(): pl.pallas_call(kernel, out_shape=jax.ShapeDtypeStruct(earlier_blocks.shap...  89.7 us
    unnamed x3, local copies, waits for them, and re-layouts  2.12 us

profile of v3, /device:TPU:1, one launch (start us, length us, event | category | flops | bytes accessed | tf_op | source)
XLA Modules:
  0.0 91.8 jit_solution(7663003646741716805)
XLA Ops:
  0.0 0.0 copy-start
  0.0 1.1 %copy-done = f32[1,50,4096]{2,0,1:T(1,128)S(1)} copy-done((f32[1,50,4096]{2,0,1:T(1,128)S(1)}, f32[1,50,4096]{2,0,1:T(1,128)}, u32[]{:S(2)}) %copy-start) | copy-done | bytes 819224
  1.1 89.7 %shard_map.28 = f32[1,512,512]{2,1,0:T(8,128)S(1)} custom-call(f32[1600,128]{1,0:T(8,128)S(1)} %bitcast.1, f32[1,512,512]{2,1,0:T(8,128)} %earlier_hbm.1), custom_call_target="tpu_custom_call" | custom-call | flops 5033164800 | bytes 3145728 | tf_op jit(solution)/shard_map/pallas_call | solution.py:296
  90.8 1.0 %copy.4 = f32[1,512,512]{2,1,0:T(8,128)} copy(f32[1,512,512]{2,1,0:T(8,128)S(1)} %shard_map.28) | data formatting | bytes 2097152
Async XLA Ops:
  0.0 1.1 %copy-start = (f32[1,50,4096]{2,0,1:T(1,128)S(1)}, f32[1,50,4096]{2,0,1:T(1,128)}, u32[]{:S(2)}) copy-start(f32[1,50,4096]{2,0,1:T(1,128)} %param.2) | copy-start | bytes 2457604

commit v4 on v3

--- a/solution.py
+++ b/solution.py
@@ -18,7 +18,6 @@
 OWN = 64
 CHUNKS = 4
 PART = OWN // CHUNKS
-HALVED = (2,)
 WIDTH = 512
 
 GROUPS = (
@@ -105,7 +104,8 @@
             col_send[j, pl.ds(8 * i + 4, 4), :] = half[pl.ds(32 * i + 16 + 4 * n, 4), :]
             row_send[j, pl.ds(8 * i, 8), :] = half[pl.ds(32 * i + m, 8, stride=4), :]
 
-    prepare(1)
+    for j in (1, 3, 2, 0):
+        prepare(j)
     pl.semaphore_wait(barrier, len(peers))
 
     sends = []
@@ -114,43 +114,34 @@
         copy.start()
         sends.append(copy)
 
+    def drain(left, most):
+        for _ in range(min(most, len(sends) - left)):
+            sends.pop(0).wait_send()
+
     for j in (1, 3, 2):
-        if j != 1:
-            prepare(j)
         go(remote(col_send.at[j], slot(col_buf, 4 - j, 0), c_ssem.at[j, 0], c_rsem.at[4 - j, 0], device(dx=j)))
         go(remote(row_send.at[j], slot(row_buf, 0, 4 - j), r_ssem.at[j, 0], r_rsem.at[0, 4 - j], device(dy=j)))
-    prepare(0)
     slot(col_buf, 0, 0)[...] = col_send[0]
     slot(row_buf, 0, 0)[...] = row_send[0]
 
     def spread(a):
-        for part, up, down in ((0, 1, 2), (1, 5, 6)) if a in HALVED else ((None, 1, 2),):
-            other = None if part is None else 1 - part
-            up_to = 3 if up == 1 else 5
-            down_to = 1 if down == 2 else 6
-            go(remote(slot(col_buf, a, 0, part), slot(col_buf, a, 3, part), c_ssem.at[a, up], c_rsem.at[a, up_to], device(dy=1)))
-            go(remote(slot(row_buf, 0, a, part), slot(row_buf, 3, a, part), r_ssem.at[a, up], r_rsem.at[up_to, a], device(dx=1)))
-            go(remote(slot(col_buf, a, 0, other), slot(col_buf, a, 1, other), c_ssem.at[a, down], c_rsem.at[a, down_to], device(dy=3)))
-            go(remote(slot(row_buf, 0, a, other), slot(row_buf, 1, a, other), r_ssem.at[a, down], r_rsem.at[down_to, a], device(dx=3)))
+        go(remote(slot(col_buf, a, 0), slot(col_buf, a, 3), c_ssem.at[a, 1], c_rsem.at[a, 3], device(dy=1)))
+        go(remote(slot(row_buf, 0, a), slot(row_buf, 3, a), r_ssem.at[a, 1], r_rsem.at[3, a], device(dx=1)))
+        go(remote(slot(col_buf, a, 0), slot(col_buf, a, 1), c_ssem.at[a, 2], c_rsem.at[a, 1], device(dy=3)))
+        go(remote(slot(row_buf, 0, a), slot(row_buf, 1, a), r_ssem.at[a, 2], r_rsem.at[1, a], device(dx=3)))
 
     def arrived(dst, rsem):
         remote(dst, dst, rsem, rsem, device(dy=1)).wait_recv()
 
     def forward(a):
-        low, high = (0, 1) if a in HALVED else (None, None)
-        arrived(slot(col_buf, a, 3, low), c_rsem.at[a, 3])
+        arrived(slot(col_buf, a, 3), c_rsem.at[a, 3])
         go(remote(slot(col_buf, a, 3, 0), slot(col_buf, a, 2, 0), c_ssem.at[a, 3], c_rsem.at[a, 2], device(dy=1)))
-        arrived(slot(row_buf, 3, a, low), r_rsem.at[3, a])
+        arrived(slot(row_buf, 3, a), r_rsem.at[3, a])
         go(remote(slot(row_buf, 3, a, 0), slot(row_buf, 2, a, 0), r_ssem.at[a, 3], r_rsem.at[2, a], device(dx=1)))
-        arrived(slot(col_buf, a, 1, high), c_rsem.at[a, 1])
+        arrived(slot(col_buf, a, 1), c_rsem.at[a, 1])
         go(remote(slot(col_buf, a, 1, 1), slot(col_buf, a, 2, 1), c_ssem.at[a, 4], c_rsem.at[a, 4], device(dy=3)))
-        arrived(slot(row_buf, 1, a, high), r_rsem.at[1, a])
+        arrived(slot(row_buf, 1, a), r_rsem.at[1, a])
         go(remote(slot(row_buf, 1, a, 1), slot(row_buf, 2, a, 1), r_ssem.at[a, 4], r_rsem.at[4, a], device(dx=3)))
-        if a in HALVED:
-            arrived(slot(col_buf, a, 3, 1), c_rsem.at[a, 5])
-            arrived(slot(row_buf, 3, a, 1), r_rsem.at[5, a])
-            arrived(slot(col_buf, a, 1, 0), c_rsem.at[a, 6])
-            arrived(slot(row_buf, 1, a, 0), r_rsem.at[6, a])
 
     def finish(a):
         arrived(slot(col_buf, a, 2, 0), c_rsem.at[a, 2])
@@ -217,12 +208,11 @@
     other = pl.ds(pl.multiple_of((1 - k) * OWN, OWN), OWN)
 
     def last(m):
-        for j in range(4):
-            acc = product(slice(256 * m, 256 * m + 256), slice(256 * j, 256 * j + 256))
-            cols = slice((j % 2) * 256, (j % 2) * 256 + 256)
-            for n in range(2):
-                tile[4 * m + 2 * n + j // 2, :, cols] += acc[128 * n : 128 * n + 128]
-        for n in (2 * m, 2 * m + 1):
+        for j in range(2):
+            acc = product(slice(512 * m, 512 * m + 512), slice(512 * j, 512 * j + 512))
+            for n in range(4):
+                tile[8 * m + 2 * n + j] += acc[128 * n : 128 * n + 128]
+        for n in range(4 * m, 4 * m + 4):
             go(remote(tile.at[pl.ds(2 * n, 2), other, :], sibling_tile.at[pl.ds(2 * n, 2)], s_ssem.at[n], s_rsem.at[n], device(dk=1)))
 
     def sibling_arrived(n):
@@ -251,20 +241,20 @@
                 go(remote(ring_send.at[way, s, ch], ring_recv.at[way, s, ch], ring_ssem.at[way, s, ch], ring_rsem.at[way, s, ch], to))
 
     last(0)
-    last(1)
     sibling_arrived(0)
     sibling_arrived(1)
     step(0)
-    last(2)
+    last(1)
     sibling_arrived(2)
     step(1)
-    last(3)
     sibling_arrived(3)
     step(2)
+    drain(16, 24)
     for s in range(3, 8):
         if s < 7:
             sibling_arrived(s + 1)
         step(s)
+        drain(8, 24)
 
     load_earlier.wait()
     for ch in range(CHUNKS):
@@ -313,10 +303,10 @@
             pltpu.VMEM((2, 8, CHUNKS, PART, WIDTH), F32),
             pltpu.VMEM((2, 8, CHUNKS, PART, WIDTH), F32),
             dma((1,)),
-            dma((4, 7)),
-            dma((4, 7)),
-            dma((4, 7)),
-            dma((7, 5)),
+            dma((4, 5)),
+            dma((4, 5)),
+            dma((4, 5)),
+            dma((5, 5)),
             dma((8,)),
             dma((8,)),
             dma((2, 8, CHUNKS)),

time: 91.9 us -> 91.2 us (level)
  no operation moved by 1% of the time
where the time goes in v4:
time: 91.2 us; the launch traced here: 91 us
  Pallas kernels  88.9 us (97%)
  local copies, waits for them, and re-layouts  2.12 us (2%)
    pallas_call x1, Pallas kernels, body(): pl.pallas_call(kernel, out_shape=jax.ShapeDtypeStruct(earlier_blocks.shap...  88.9 us
    unnamed x3, local copies, waits for them, and re-layouts  2.12 us

profile of v4, /device:TPU:1, one launch (start us, length us, event | category | flops | bytes accessed | tf_op | source)
XLA Modules:
  0.0 91.0 jit_solution(4677262714646614442)
XLA Ops:
  0.0 0.0 copy-start
  0.0 1.1 %copy-done = f32[1,50,4096]{2,0,1:T(1,128)S(1)} copy-done((f32[1,50,4096]{2,0,1:T(1,128)S(1)}, f32[1,50,4096]{2,0,1:T(1,128)}, u32[]{:S(2)}) %copy-start) | copy-done | bytes 819224
  1.1 88.9 %shard_map.28 = f32[1,512,512]{2,1,0:T(8,128)S(1)} custom-call(f32[1600,128]{1,0:T(8,128)S(1)} %bitcast.1, f32[1,512,512]{2,1,0:T(8,128)} %earlier_hbm.1), custom_call_target="tpu_custom_call" | custom-call | flops 5033164800 | bytes 3145728 | tf_op jit(solution)/shard_map/pallas_call | solution.py:286
  90.0 1.0 %copy.4 = f32[1,512,512]{2,1,0:T(8,128)} copy(f32[1,512,512]{2,1,0:T(8,128)S(1)} %shard_map.28) | data formatting | bytes 2097152
Async XLA Ops:
  0.0 1.1 %copy-start = (f32[1,50,4096]{2,0,1:T(1,128)S(1)}, f32[1,50,4096]{2,0,1:T(1,128)}, u32[]{:S(2)}) copy-start(f32[1,50,4096]{2,0,1:T(1,128)} %param.2) | copy-start | bytes 2457604

commit v5 on v4

--- a/solution.py
+++ b/solution.py
@@ -14,6 +14,7 @@
 PIECE = ROWS * 8
 HALF = 25 * 8
 DEPTH = 256
+LAST = 128
 QUARTER = 128
 OWN = 64
 CHUNKS = 4
@@ -23,8 +24,8 @@
 GROUPS = (
     ((0, 0), (0, 3), (3, 0), (3, 3)),
     ((0, 1), (1, 0), (1, 1), (1, 3), (3, 1)),
-    ((0, 2), (2, 0), (3, 2), (2, 3)),
-    ((1, 2), (2, 1), (2, 2)),
+    ((0, 2), (2, 0), (3, 2), (2, 3), (1, 2)),
+    ((2, 1), (2, 2)),
 )
 PLACE = {source: (g, i) for g, group in enumerate(GROUPS) for i, source in enumerate(group)}
 OFFSETS = (4, 3, 5, 2, 6, 1, 7, 0)
@@ -149,23 +150,23 @@
         arrived(slot(col_buf, a, 2, 1), c_rsem.at[a, 4])
         arrived(slot(row_buf, 2, a, 1), r_rsem.at[4, a])
 
-    def split(g):
+    def split(g, depth=DEPTH):
         for n in range(8):
-            v = col_buf[g, pl.ds(n, DEPTH, stride=8), :]
+            v = col_buf[g, pl.ds(n, depth, stride=8), :]
             hi = v.astype(BF16)
-            col_hi[:, 128 * n : 128 * n + 128] = hi
-            col_lo[:, 128 * n : 128 * n + 128] = (v - hi.astype(F32)).astype(BF16)
+            col_hi[:depth, 128 * n : 128 * n + 128] = hi
+            col_lo[:depth, 128 * n : 128 * n + 128] = (v - hi.astype(F32)).astype(BF16)
             offset = odd * ((8 - OFFSETS[n]) % 8) + (1 - odd) * OFFSETS[n]
             u = lax.rem(z // 2 + offset, 8)
-            v = row_buf[g, pl.ds(u, DEPTH, stride=8), :].T
+            v = row_buf[g, pl.ds(u, depth, stride=8), :].T
             hi = v.astype(BF16)
-            row_hi[128 * n : 128 * n + 128, :] = hi
-            row_lo[128 * n : 128 * n + 128, :] = (v - hi.astype(F32)).astype(BF16)
-
-    def product(rows, cols):
-        acc = jnp.dot(row_lo[rows, :], col_hi[:, cols], preferred_element_type=F32)
-        acc += jnp.dot(row_hi[rows, :], col_lo[:, cols], preferred_element_type=F32)
-        acc += jnp.dot(row_hi[rows, :], col_hi[:, cols], preferred_element_type=F32)
+            row_hi[128 * n : 128 * n + 128, :depth] = hi
+            row_lo[128 * n : 128 * n + 128, :depth] = (v - hi.astype(F32)).astype(BF16)
+
+    def product(rows, cols, depth=DEPTH):
+        acc = jnp.dot(row_lo[rows, :depth], col_hi[:depth, cols], preferred_element_type=F32)
+        acc += jnp.dot(row_hi[rows, :depth], col_lo[:depth, cols], preferred_element_type=F32)
+        acc += jnp.dot(row_hi[rows, :depth], col_hi[:depth, cols], preferred_element_type=F32)
         return acc
 
     def multiply(g):
@@ -200,16 +201,16 @@
     forward(2)
     finish(0)
     finish(3)
+    finish(1)
     multiply(2)
-    finish(1)
     finish(2)
-    split(3)
+    split(3, LAST)
 
     other = pl.ds(pl.multiple_of((1 - k) * OWN, OWN), OWN)
 
     def last(m):
         for j in range(2):
-            acc = product(slice(512 * m, 512 * m + 512), slice(512 * j, 512 * j + 512))
+            acc = product(slice(512 * m, 512 * m + 512), slice(512 * j, 512 * j + 512), LAST)
             for n in range(4):
                 tile[8 * m + 2 * n + j] += acc[128 * n : 128 * n + 128]
         for n in range(4 * m, 4 * m + 4):

time: 91.2 us -> 92.7 us (1.016)
  Pallas kernels: 88.9 us -> 90.4 us
    pallas_call x1, Pallas kernels: 88.9 us -> 90.4 us  [body(): pl.pallas_call(kernel, out_shape=jax.ShapeDtypeStruct(earlier_blocks.shap...]
where the time goes in v5:
time: 92.7 us; the launch traced here: 92.5 us
  Pallas kernels  90.4 us (98%)
  local copies, waits for them, and re-layouts  2.12 us (2%)
    pallas_call x1, Pallas kernels, body(): pl.pallas_call(kernel, out_shape=jax.ShapeDtypeStruct(earlier_blocks.shap...  90.4 us
    unnamed x3, local copies, waits for them, and re-layouts  2.12 us

profile of v5, /device:TPU:1, one launch (start us, length us, event | category | flops | bytes accessed | tf_op | source)
XLA Modules:
  0.0 92.5 jit_solution(14092528618492508749)
XLA Ops:
  0.0 0.0 copy-start
  0.0 1.1 %copy-done = f32[1,50,4096]{2,0,1:T(1,128)S(1)} copy-done((f32[1,50,4096]{2,0,1:T(1,128)S(1)}, f32[1,50,4096]{2,0,1:T(1,128)}, u32[]{:S(2)}) %copy-start) | copy-done | bytes 819224
  1.1 90.4 %shard_map.28 = f32[1,512,512]{2,1,0:T(8,128)S(1)} custom-call(f32[1600,128]{1,0:T(8,128)S(1)} %bitcast.1, f32[1,512,512]{2,1,0:T(8,128)} %earlier_hbm.1), custom_call_target="tpu_custom_call" | custom-call | flops 5033164800 | bytes 3145728 | tf_op jit(solution)/shard_map/pallas_call | solution.py:287
  91.5 1.0 %copy.4 = f32[1,512,512]{2,1,0:T(8,128)} copy(f32[1,512,512]{2,1,0:T(8,128)S(1)} %shard_map.28) | data formatting | bytes 2097152
Async XLA Ops:
  0.0 1.1 %copy-start = (f32[1,50,4096]{2,0,1:T(1,128)S(1)}, f32[1,50,4096]{2,0,1:T(1,128)}, u32[]{:S(2)}) copy-start(f32[1,50,4096]{2,0,1:T(1,128)} %param.2) | copy-start | bytes 2457604

commit v6 on v4

--- a/solution.py
+++ b/solution.py
@@ -79,7 +79,7 @@
         start = lax.rem(y + dy, NY) * QUARTER + lax.rem(k + dk, NK) * OWN
         if chunk is None:
             return pl.ds(pl.multiple_of(start, OWN), OWN)
-        return pl.ds(pl.multiple_of(start + chunk * PART, PART), PART)
+        return pl.ds(pl.multiple_of(start + chunk * 2 * PART, 2 * PART), 2 * PART)
 
     load_earlier = pltpu.make_async_copy(earlier_hbm.at[0, rows_of(0, 0), :], earlier, in_sem.at[0])
     load_earlier.start()
@@ -262,19 +262,22 @@
         for way in range(2):
             arrived(ring_recv.at[way, 7, ch], ring_rsem.at[way, 7, ch])
             total += ring_recv[way, 7, ch]
-        here = rows_of(0, 0, ch)
-        out_ref[0, here, :] = total
-        for j in (2, 1, 3):
-            go(remote(out_ref.at[0, here, :], out_ref.at[0, here, :], o_ssem.at[j, ch], o_rsem.at[4 - j, ch], device(dy=j)))
-        go(remote(out_ref.at[0, here, :], out_ref.at[0, here, :], o_ssem.at[4, ch], o_rsem.at[4, ch], device(dk=1)))
-    for ch in range(CHUNKS):
+        start = y * QUARTER + k * OWN + ch * PART
+        out_ref[0, pl.ds(pl.multiple_of(start, PART), PART), :] = total
+        if ch % 2 == 1:
+            part = ch // 2
+            block = out_ref.at[0, rows_of(0, 0, part), :]
+            for j in (2, 1, 3):
+                go(remote(block, block, o_ssem.at[j, part], o_rsem.at[4 - j, part], device(dy=j)))
+            go(remote(block, block, o_ssem.at[4, part], o_rsem.at[4, part], device(dk=1)))
+    for part in range(CHUNKS // 2):
         for j in (3, 1, 2):
-            rows = rows_of(j, 0, ch)
-            arrived(out_ref.at[0, rows, :], o_rsem.at[j, ch])
-            go(remote(out_ref.at[0, rows, :], out_ref.at[0, rows, :], o_ssem.at[4 + j, ch], o_rsem.at[4 + j, ch], device(dk=1)))
-    for ch in range(CHUNKS):
+            block = out_ref.at[0, rows_of(j, 0, part), :]
+            arrived(block, o_rsem.at[j, part])
+            go(remote(block, block, o_ssem.at[4 + j, part], o_rsem.at[4 + j, part], device(dk=1)))
+    for part in range(CHUNKS // 2):
         for j in range(4):
-            arrived(out_ref.at[0, rows_of(j, 1, ch), :], o_rsem.at[4 + j, ch])
+            arrived(out_ref.at[0, rows_of(j, 1, part), :], o_rsem.at[4 + j, part])
     for copy in sends:
         copy.wait_send()
 
@@ -311,8 +314,8 @@
             dma((8,)),
             dma((2, 8, CHUNKS)),
             dma((2, 8, CHUNKS)),
-            dma((8, CHUNKS)),
-            dma((8, CHUNKS)),
+            dma((8, CHUNKS // 2)),
+            dma((8, CHUNKS // 2)),
         ],
         compiler_params=pltpu.CompilerParams(
             collective_id=0, has_side_effects=True, vmem_limit_bytes=52 * 2**20

time: 91.2 us -> 91.8 us (level)
  no operation moved by 1% of the time
where the time goes in v6:
time: 91.8 us; the launch traced here: 91.6 us
  Pallas kernels  89.5 us (97%)
  local copies, waits for them, and re-layouts  2.12 us (2%)
    pallas_call x1, Pallas kernels, body(): pl.pallas_call(kernel, out_shape=jax.ShapeDtypeStruct(earlier_blocks.shap...  89.5 us
    unnamed x3, local copies, waits for them, and re-layouts  2.12 us

profile of v6, /device:TPU:1, one launch (start us, length us, event | category | flops | bytes accessed | tf_op | source)
XLA Modules:
  0.0 91.6 jit_solution(3823234047533383305)
XLA Ops:
  0.0 0.0 copy-start
  0.0 1.1 %copy-done = f32[1,50,4096]{2,0,1:T(1,128)S(1)} copy-done((f32[1,50,4096]{2,0,1:T(1,128)S(1)}, f32[1,50,4096]{2,0,1:T(1,128)}, u32[]{:S(2)}) %copy-start) | copy-done | bytes 819224
  1.1 89.5 %shard_map.28 = f32[1,512,512]{2,1,0:T(8,128)S(1)} custom-call(f32[1600,128]{1,0:T(8,128)S(1)} %bitcast.1, f32[1,512,512]{2,1,0:T(8,128)} %earlier_hbm.1), custom_call_target="tpu_custom_call" | custom-call | flops 5033164800 | bytes 3145728 | tf_op jit(solution)/shard_map/pallas_call | solution.py:289
  90.6 1.0 %copy.4 = f32[1,512,512]{2,1,0:T(8,128)} copy(f32[1,512,512]{2,1,0:T(8,128)S(1)} %shard_map.28) | data formatting | bytes 2097152
Async XLA Ops:
  0.0 1.1 %copy-start = (f32[1,50,4096]{2,0,1:T(1,128)S(1)}, f32[1,50,4096]{2,0,1:T(1,128)}, u32[]{:S(2)}) copy-start(f32[1,50,4096]{2,0,1:T(1,128)} %param.2) | copy-start | bytes 2457604
